TPU v7x, 32 devices: a whole 2x2x4 slice. The times are simulated.
32 devices in a mesh: groups: 2 (over x), ctx: 16 (over z, y, core).
Axes of the slice: x: 2, y: 2, z: 4, core: 2. Of those that a mesh axis runs over, the one named last changes fastest.
Arguments:
- layer_normed_input: bfloat16 [4096, 4096], P(('groups', 'ctx')), parts along dimension 0, may hold values from -6 to 6
- queries: bfloat16 [4096, 2048], P(('groups', 'ctx')), parts along dimension 0, may hold values from -300 to 300
- keys: bfloat16 [4096, 512], P(('groups', 'ctx')), parts along dimension 0, may hold values from -4 to 4
- output_gradient: bfloat16 [4096, 2048], P(('groups', 'ctx')), parts along dimension 0, may hold values from -6 to 6
- adapter_down: bfloat16 [4096, 128], replicated, may hold values from -0.09375 to 0.09375
- adapter_up: bfloat16 [128, 512], replicated, may hold values from -0.5 to 0.5
- down_sign_bits: int32 [4096, 32], replicated, may hold values from 0 to 1
- up_sign_bits: int32 [512, 32], replicated, may hold values from 0 to 1
- block_position_order: int32 [64], P('groups'), parts along dimension 0, may hold values from 0 to 31, each once
- document_lengths: int32 [8], P('groups'), parts along dimension 0, may hold values from 1 to 768, 2048 in all
Outputs:
- features: float32 [8, 8192], P('groups'), parts along dimension 0
There are 2 independent parts, one for each index of `groups`. A program takes and returns all parts, laid end to end along the dimension named above; an argument that names none is the same for every part. Nothing has to cross between parts.
Inputs may be any that keep to these rules, and one draw needn't show every extreme that they name: Block of rows k of the pack (rows k * 64 to (k + 1) * 64 - 1) holds positions block_position_order[k] * 64 onward; every block of positions appears once. `document_lengths`: the lengths are positive and sum to 2048; the longest is exactly 768.
All inputs are finite; a program needn't handle non-finite values.
Results may differ from a plain program's by a relative error of at most 0.0038.
Values may be sent and summed in bfloat16 or wider, within the bound.
A program may use at most 64 MiB of HBM per device.

v0:
```python
import math

import jax
import jax.numpy as jnp
from jax import lax
from jax.sharding import PartitionSpec as P

HEAD_SIZE = 128
HEADS = 16
KEY_VALUE_HEADS = 4
ADAPTER_RANK = 128
FEAT_A = 32
FEAT_B = 32
DOCS = 4
BLOCK_ROWS = 64


norm_eps = 1e-06
span_cap = 512
far_low = -1e30


def unit_rows(values):
    return values * lax.rsqrt(jnp.mean(values * values, axis=-1, keepdims=True) + norm_eps)


def head_scores(query_heads, key_block):
    raw_scores = jnp.einsum(
        "tkgd,ckd->kgtc", query_heads, key_block, preferred_element_type=jnp.float32
    )
    return raw_scores * (1.0 / math.sqrt(HEAD_SIZE))


def per_device(
    layer_normed_input,
    queries,
    keys,
    output_gradient,
    adapter_down,
    adapter_up,
    down_sign_bits,
    up_sign_bits,
    block_position_order,
    document_lengths,
):
    shard_count = lax.axis_size("ctx")
    shard_index = lax.axis_index("ctx")
    local_rows = layer_normed_input.shape[0]
    all_rows = local_rows * shard_count
    group_size = HEADS // KEY_VALUE_HEADS
    value_width = KEY_VALUE_HEADS * HEAD_SIZE
    offsets = jnp.arange(BLOCK_ROWS, dtype=jnp.int32)
    all_positions = (block_position_order[:, None] * BLOCK_ROWS + offsets[None, :]).reshape(
        all_rows
    )
    doc_ends = jnp.cumsum(document_lengths)[: DOCS - 1]
    all_docs = jnp.sum((all_positions[:, None] >= doc_ends[None, :]).astype(jnp.int32), axis=1)
    my_positions = lax.dynamic_slice_in_dim(all_positions, shard_index * local_rows, local_rows)
    my_docs = lax.dynamic_slice_in_dim(all_docs, shard_index * local_rows, local_rows)
    query_heads = queries.reshape(local_rows, KEY_VALUE_HEADS, group_size, HEAD_SIZE)
    grad_heads = output_gradient.reshape(local_rows, KEY_VALUE_HEADS, group_size, HEAD_SIZE)
    key_rows = lax.all_gather(keys, "ctx", axis=0, tiled=True)
    key_span = math.gcd(all_rows, span_cap)
    span_count = all_rows // key_span

    def allowed_pairs(key_pos, key_docs):
        return (my_docs[:, None] == key_docs[None, :]) & (key_pos[None, :] <= my_positions[:, None])

    def stats_step(stat_carry, block_items):
        running_top, running_sum = stat_carry
        key_block, key_pos, key_docs = block_items
        allowed = allowed_pairs(key_pos, key_docs)

        def update(ignored):
            score_block = head_scores(query_heads, key_block)
            new_top = jnp.maximum(
                running_top, jnp.max(jnp.where(allowed, score_block, -jnp.inf), axis=-1)
            )
            fresh_sum = jnp.sum(
                jnp.where(allowed, jnp.exp(score_block - new_top[..., None]), 0.0), axis=-1
            )
            return (new_top, running_sum * jnp.exp(running_top - new_top) + fresh_sum)

        return (
            lax.cond(jnp.any(allowed), update, lambda ignored: (running_top, running_sum), 0),
            None,
        )

    initial = (
        jnp.full((KEY_VALUE_HEADS, group_size, local_rows), far_low, jnp.float32),
        jnp.zeros((KEY_VALUE_HEADS, group_size, local_rows), jnp.float32),
    )
    stat_items = (
        key_rows.reshape(span_count, key_span, KEY_VALUE_HEADS, HEAD_SIZE),
        all_positions.reshape(span_count, key_span),
        all_docs.reshape(span_count, key_span),
    )
    (running_top, running_sum), ignored_stats = lax.scan(stats_step, initial, stat_items)
    log_total = running_top + jnp.log(running_sum)

    def make_term(finish, out_width):
        piece_rows = math.gcd(local_rows * lax.axis_size("ctx"), span_cap)
        piece_count = local_rows * lax.axis_size("ctx") // piece_rows

        def piece_step(unused_carry, block_items):
            key_block, key_pos, key_docs = block_items
            allowed = allowed_pairs(key_pos, key_docs)

            def compute(unused):
                score_block = head_scores(query_heads, key_block)
                weights = jnp.where(
                    allowed, jnp.exp(score_block - log_total[..., None]), 0.0
                ).astype(jnp.bfloat16)
                addend = jnp.einsum(
                    "kgtc,tkgd->ckd", weights, grad_heads, preferred_element_type=jnp.float32
                )
                return finish(addend.reshape(piece_rows, value_width))

            empty = lambda unused: jnp.zeros((piece_rows, out_width), jnp.float32)
            return (unused_carry, lax.cond(jnp.any(allowed), compute, empty, 0))

        piece_items = (
            key_rows.reshape(piece_count, piece_rows, KEY_VALUE_HEADS, HEAD_SIZE),
            all_positions.reshape(piece_count, piece_rows),
            all_docs.reshape(piece_count, piece_rows),
        )
        unused_final, pieces = lax.scan(piece_step, 0, piece_items)
        return pieces.reshape(local_rows * lax.axis_size("ctx"), out_width)

    low_rank_term = jnp.dot(
        layer_normed_input, adapter_down, preferred_element_type=jnp.float32
    ).astype(jnp.bfloat16)
    member = (my_docs[:, None] == jnp.arange(DOCS, dtype=jnp.int32)[None, :]).astype(jnp.float32)
    low_docs = (member[:, :, None] * low_rank_term.astype(jnp.float32)[:, None, :]).reshape(
        local_rows, DOCS * ADAPTER_RANK
    )
    over_rows = (((0,), (0,)), ((), ()))
    value_gradient_sum = lax.psum_scatter(
        make_term(lambda addend: addend, value_width), "ctx", scatter_dimension=0, tiled=True
    )
    backward_step = lax.dot_general(
        value_gradient_sum,
        adapter_up.astype(jnp.float32),
        (((1,), (1,)), ((), ())),
        precision=lax.Precision.HIGHEST,
    )
    back_docs = (member[:, :, None] * backward_step[:, None, :]).reshape(
        local_rows, DOCS * ADAPTER_RANK
    )
    signs_a = (2 * down_sign_bits - 1).astype(jnp.bfloat16)
    signs_b = (2 * up_sign_bits - 1).astype(jnp.float32)
    proj_in = jnp.dot(layer_normed_input, signs_a, preferred_element_type=jnp.float32)
    proj_val = jnp.dot(value_gradient_sum, signs_b, precision=lax.Precision.HIGHEST)
    part_a = lax.dot_general(proj_in, back_docs, over_rows, precision=lax.Precision.HIGHEST)
    part_b = lax.dot_general(low_docs, proj_val, over_rows, precision=lax.Precision.HIGHEST)
    raw_a, raw_b = lax.psum((part_a, part_b), "ctx")
    feats_a = (
        raw_a.reshape(FEAT_A, DOCS, ADAPTER_RANK)
        .transpose(1, 0, 2)
        .reshape(DOCS, FEAT_A * ADAPTER_RANK)
    )
    feats_b = raw_b.reshape(DOCS, ADAPTER_RANK * FEAT_B)
    return jnp.concatenate([unit_rows(feats_a), unit_rows(feats_b)], axis=1)


def solution(mesh):
    placed = (
        P(("groups", "ctx"), None),
        P(("groups", "ctx"), None),
        P(("groups", "ctx"), None),
        P(("groups", "ctx"), None),
        P(),
        P(),
        P(),
        P(),
        P("groups"),
        P("groups"),
    )
    return jax.shard_map(
        per_device, mesh=mesh, in_specs=placed, out_specs=P("groups", None), check_vma=False
    )
```

profile of v0, /device:TPU:0, one launch (start us, length us, event | category | flops | bytes accessed | tf_op | source)
XLA Modules:
  0.0 272.3 jit_solution(1706026300559451387)
XLA Ops:
  9.5 1.3 copy.25
  10.9 1.0 copy.30
  11.9 2.1 copy.28
  14.0 39.7 %all-gather.2.cloned.1.call-done = bf16[2048,512]{1,0:T(8,128)(2,1)} async-done(((bf16[128,512]{1,0:T(8,128)(2,1)}), bf16[2048,512]{1,0:T(8,128)(2,1)}) %all-gather.2.cloned.1.call-update) | async-done | bytes 2097168 | tf_op jit(solution)/shard_map/all_gather | solution.py:62
  53.7 2.5 reshape.114
  56.2 1.7 copy.29
  57.9 17.3 %while.22 = (s32[]{:T(128)}, f32[4,4,128]{2,1,0:T(4,128)S(1)}, f32[4,4,128]{2,1,0:T(4,128)S(1)}, s32[128]{0:T(128)S(1)}, s32[4,512]{1,0:T(4,128)S(1)}, /*index=5...) while((s32[]{:T(128)}, f32[4,4,128]{2,1,0:T(4,128)S(1)}, ...), condition=%wide.region_8.9_spmd, body=%wide.region_2.8_spmd.sunk | while | flops 276041728 | bytes 9754311 | solution.py:98
  59.4 2.9 %conditional.4 = ((f32[4,4,128]{2,1,0:T(4,128)S(1)}, f32[4,4,128]{2,1,0:T(4,128)S(1)})) conditional(s32[]{:T(128)} %convert_element_type.54, (f32[4,4,128]{2,1,0:T(4,128)S(1)}, f32[4,4,128]{2,1,0:T(4,128)S(1)}) %tuple.70, (pred[128,512]{0,1:T(8,128)(4,1)S(1)}, bf16[4,512,4,128]{3,1,2,0:T(8,128)(2,1)}, s32[]{:T(128)}, ...), branch_computations={%region_4.4_spmd, %region_5.7_spmd} | conditional | flops 275779584 | bytes 9675288 | solution.py:85
  59.4 1.9 fusion
  63.7 2.9 %conditional.4 = ((f32[4,4,128]{2,1,0:T(4,128)S(1)}, f32[4,4,128]{2,1,0:T(4,128)S(1)})) conditional(s32[]{:T(128)} %convert_element_type.54, (f32[4,4,128]{2,1,0:T(4,128)S(1)}, f32[4,4,128]{2,1,0:T(4,128)S(1)}) %tuple.70, (pred[128,512]{0,1:T(8,128)(4,1)S(1)}, bf16[4,512,4,128]{3,1,2,0:T(8,128)(2,1)}, s32[]{:T(128)}, ...), branch_computations={%region_4.4_spmd, %region_5.7_spmd} | conditional | flops 275779584 | bytes 9675288 | solution.py:85
  63.7 1.9 fusion
  68.0 2.9 %conditional.4 = ((f32[4,4,128]{2,1,0:T(4,128)S(1)}, f32[4,4,128]{2,1,0:T(4,128)S(1)})) conditional(s32[]{:T(128)} %convert_element_type.54, (f32[4,4,128]{2,1,0:T(4,128)S(1)}, f32[4,4,128]{2,1,0:T(4,128)S(1)}) %tuple.70, (pred[128,512]{0,1:T(8,128)(4,1)S(1)}, bf16[4,512,4,128]{3,1,2,0:T(8,128)(2,1)}, s32[]{:T(128)}, ...), branch_computations={%region_4.4_spmd, %region_5.7_spmd} | conditional | flops 275779584 | bytes 9675288 | solution.py:85
  68.0 1.9 fusion
  72.3 2.9 %conditional.4 = ((f32[4,4,128]{2,1,0:T(4,128)S(1)}, f32[4,4,128]{2,1,0:T(4,128)S(1)})) conditional(s32[]{:T(128)} %convert_element_type.54, (f32[4,4,128]{2,1,0:T(4,128)S(1)}, f32[4,4,128]{2,1,0:T(4,128)S(1)}) %tuple.70, (pred[128,512]{0,1:T(8,128)(4,1)S(1)}, bf16[4,512,4,128]{3,1,2,0:T(8,128)(2,1)}, s32[]{:T(128)}, ...), branch_computations={%region_4.4_spmd, %region_5.7_spmd} | conditional | flops 275779584 | bytes 9675288 | solution.py:85
  72.3 1.9 fusion
  75.2 23.7 %while.23 = (s32[]{:T(128)}, f32[4,512,512]{2,1,0:T(8,128)}, s32[128]{0:T(128)S(1)}, s32[4,512]{1,0:T(4,128)S(1)}, s32[4,512]{1,0:T(4,128)S(1)}, /*index=5*/s32[...) while((s32[]{:T(128)}, f32[4,512,512]{2,1,0:T(8,128)}, ...), condition=%wide.region_13.14_spmd, body=%wide.region_9.13_spmd.sunk | while | flops 541327360 | bytes 6969519 | solution.py:127
  76.8 2.9 %conditional.5 = (f32[1,512,512]{1,2,0:T(8,128)S(1)}) conditional(s32[]{:T(128)} %convert_element_type.55, () %tuple.75, (pred[128,512]{0,1:T(8,128)(4,1)S(1)}, bf16[4,512,4,128]{3,1,2,0:T(8,128)(2,1)}, s32[]{:T(128)}, bf16[128,4,4,128]{3,0,2,1:T(8,128)(2,1)}, f32[4,4,128]{2,1,0:T(4,128)S(1)}, /*index=5*/bf16[128,4,4,128]{0,3,2,1:T(8,128)(2,1)}) %tuple.76), branch_computations={%region_11.11_spmd, %region_12.12_spmd} | conditional | flops 541065216 | bytes 2695688 | solution.py:120
  76.9 2.9 %fusion.11 = f32[4,512,128,1]{1,2,3,0:T(8,128)S(1)} fusion(bf16[128,4,4,128]{0,3,2,1:T(8,128)(2,1)} %get-tuple-element.166, bf16[128,4,4,128]{3,0,2,1:T(8,128)(2,1)} %get-tuple-element.164, f32[4,4,128]{2,1,0:T(4,128)S(1)} %get-tuple-element.165, pred[128,512]{0,1:T(8,128)(4,1)S(1)} %get-tuple-element.161, bf16[4,512,4,128]{3,1,2,0:T(8,128)(2,1)} %get-tuple-element.162, ...), kind=kOutput, calls=%fused_computation.18 | convolution fusion | flops 541065216 | bytes 2695680 | tf_op jit(solution)/shard_map/while/body/eval_jaxpr/cond/branch_1_fun/kgtc,tkgd->ckd/dot_general | solution.py:114
  80.1 1.1 constant_dynamic-update-slice_fusion.2
  82.7 2.9 %conditional.5 = (f32[1,512,512]{1,2,0:T(8,128)S(1)}) conditional(s32[]{:T(128)} %convert_element_type.55, () %tuple.75, (pred[128,512]{0,1:T(8,128)(4,1)S(1)}, bf16[4,512,4,128]{3,1,2,0:T(8,128)(2,1)}, s32[]{:T(128)}, bf16[128,4,4,128]{3,0,2,1:T(8,128)(2,1)}, f32[4,4,128]{2,1,0:T(4,128)S(1)}, /*index=5*/bf16[128,4,4,128]{0,3,2,1:T(8,128)(2,1)}) %tuple.76), branch_computations={%region_11.11_spmd, %region_12.12_spmd} | conditional | flops 541065216 | bytes 2695688 | solution.py:120
  82.8 2.9 %fusion.11 = f32[4,512,128,1]{1,2,3,0:T(8,128)S(1)} fusion(bf16[128,4,4,128]{0,3,2,1:T(8,128)(2,1)} %get-tuple-element.166, bf16[128,4,4,128]{3,0,2,1:T(8,128)(2,1)} %get-tuple-element.164, f32[4,4,128]{2,1,0:T(4,128)S(1)} %get-tuple-element.165, pred[128,512]{0,1:T(8,128)(4,1)S(1)} %get-tuple-element.161, bf16[4,512,4,128]{3,1,2,0:T(8,128)(2,1)} %get-tuple-element.162, ...), kind=kOutput, calls=%fused_computation.18 | convolution fusion | flops 541065216 | bytes 2695680 | tf_op jit(solution)/shard_map/while/body/eval_jaxpr/cond/branch_1_fun/kgtc,tkgd->ckd/dot_general | solution.py:114
  86.0 1.1 constant_dynamic-update-slice_fusion.2
  88.7 2.9 %conditional.5 = (f32[1,512,512]{1,2,0:T(8,128)S(1)}) conditional(s32[]{:T(128)} %convert_element_type.55, () %tuple.75, (pred[128,512]{0,1:T(8,128)(4,1)S(1)}, bf16[4,512,4,128]{3,1,2,0:T(8,128)(2,1)}, s32[]{:T(128)}, bf16[128,4,4,128]{3,0,2,1:T(8,128)(2,1)}, f32[4,4,128]{2,1,0:T(4,128)S(1)}, /*index=5*/bf16[128,4,4,128]{0,3,2,1:T(8,128)(2,1)}) %tuple.76), branch_computations={%region_11.11_spmd, %region_12.12_spmd} | conditional | flops 541065216 | bytes 2695688 | solution.py:120
  88.7 2.9 %fusion.11 = f32[4,512,128,1]{1,2,3,0:T(8,128)S(1)} fusion(bf16[128,4,4,128]{0,3,2,1:T(8,128)(2,1)} %get-tuple-element.166, bf16[128,4,4,128]{3,0,2,1:T(8,128)(2,1)} %get-tuple-element.164, f32[4,4,128]{2,1,0:T(4,128)S(1)} %get-tuple-element.165, pred[128,512]{0,1:T(8,128)(4,1)S(1)} %get-tuple-element.161, bf16[4,512,4,128]{3,1,2,0:T(8,128)(2,1)} %get-tuple-element.162, ...), kind=kOutput, calls=%fused_computation.18 | convolution fusion | flops 541065216 | bytes 2695680 | tf_op jit(solution)/shard_map/while/body/eval_jaxpr/cond/branch_1_fun/kgtc,tkgd->ckd/dot_general | solution.py:114
  91.9 1.1 constant_dynamic-update-slice_fusion.2
  94.6 2.9 %conditional.5 = (f32[1,512,512]{1,2,0:T(8,128)S(1)}) conditional(s32[]{:T(128)} %convert_element_type.55, () %tuple.75, (pred[128,512]{0,1:T(8,128)(4,1)S(1)}, bf16[4,512,4,128]{3,1,2,0:T(8,128)(2,1)}, s32[]{:T(128)}, bf16[128,4,4,128]{3,0,2,1:T(8,128)(2,1)}, f32[4,4,128]{2,1,0:T(4,128)S(1)}, /*index=5*/bf16[128,4,4,128]{0,3,2,1:T(8,128)(2,1)}) %tuple.76), branch_computations={%region_11.11_spmd, %region_12.12_spmd} | conditional | flops 541065216 | bytes 2695688 | solution.py:120
  94.6 2.9 %fusion.11 = f32[4,512,128,1]{1,2,3,0:T(8,128)S(1)} fusion(bf16[128,4,4,128]{0,3,2,1:T(8,128)(2,1)} %get-tuple-element.166, bf16[128,4,4,128]{3,0,2,1:T(8,128)(2,1)} %get-tuple-element.164, f32[4,4,128]{2,1,0:T(4,128)S(1)} %get-tuple-element.165, pred[128,512]{0,1:T(8,128)(4,1)S(1)} %get-tuple-element.161, bf16[4,512,4,128]{3,1,2,0:T(8,128)(2,1)} %get-tuple-element.162, ...), kind=kOutput, calls=%fused_computation.18 | convolution fusion | flops 541065216 | bytes 2695680 | tf_op jit(solution)/shard_map/while/body/eval_jaxpr/cond/branch_1_fun/kgtc,tkgd->ckd/dot_general | solution.py:114
  97.8 1.1 constant_dynamic-update-slice_fusion.2
  100.8 69.4 %reduce-scatter.2.cloned.1.call-done = f32[128,512]{1,0:T(8,128)} async-done(((f32[2048,512]{1,0:T(8,128)}), f32[128,512]{1,0:T(8,128)}) %reduce-scatter.2.cloned.1.call-update) | async-done | bytes 262160 | tf_op jit(solution)/shard_map/reduce_scatter | solution.py:138
  170.2 1.2 fusion.43
  172.5 1.3 fusion.30
  174.8 86.2 %all-reduce.3.cloned.1.call-done = (f32[512,32]{0,1:T(8,128)}, f32[4,32,128]{2,0,1:T(4,128)}) async-done(((f32[512,32]{0,1:T(8,128)}, f32[4,32,128]{2,0,1:T(4,128)}), (f32[512,32]{0,1:T(8,128)}, f32[4,32,128]{2,0,1:T(4,128)})) %all-reduce.3.cloned.1.call-update) | async-done | bytes 131088 | tf_op jit(solution)/shard_map/psum | solution.py:156
  (87 shorter events, 23.6 us)
Async XLA Ops:
  6.5 92.5 %copy-start = (bf16[128,4096]{1,0:T(8,128)(2,1)S(1)}, bf16[128,4096]{1,0:T(8,128)(2,1)}, u32[]{:S(2)}) copy-start(bf16[128,4096]{1,0:T(8,128)(2,1)} %param.18) | copy-start | bytes 3145732
  6.5 47.1 %all-gather.2.cloned.1.call-start = ((), (), s32[]{:S(2)}) async-start(), calls=%async_computation.1 | async-start | bytes 2228224 | tf_op jit(solution)/shard_map/all_gather | solution.py:62
  7.3 162.9 %reduce-scatter.2.cloned.1.call-start = ((), (), s32[]{:S(2)}) async-start(), calls=%async_computation.2 | async-start | bytes 4456448 | tf_op jit(solution)/shard_map/reduce_scatter | solution.py:138
  98.9 1.0 copy-start.2
  98.9 1.5 copy-start.1
  98.9 71.3 %copy-start.3 = (bf16[128,512]{1,0:T(8,128)(2,1)S(1)}, bf16[128,512]{1,0:T(8,128)(2,1)}, u32[]{:S(2)}) copy-start(bf16[128,512]{1,0:T(8,128)(2,1)} %param.23) | copy-start | bytes 393220
  98.9 73.7 %copy-start.4 = (s32[512,32]{0,1:T(8,128)S(1)}, s32[512,32]{0,1:T(8,128)}, u32[]{:S(2)}) copy-start(s32[512,32]{0,1:T(8,128)} %param.25) | copy-start | bytes 196612
  98.9 162.1 %all-reduce.3.cloned.1.call-start = ((), (), s32[]{:S(2)}) async-start(), calls=%async_computation.3 | async-start | bytes 262144 | tf_op jit(solution)/shard_map/psum | solution.py:156
Sparse Core Ops, SparseCore 0:
  9.5 44.0 all-gather.1
  99.0 71.1 reduce-scatter.1
  174.9 86.0 all-reduce.2
where the time goes:
time: 274 us; the launch traced here: 272 us
  waiting for transfers between devices  196 us (72%)
  matrix products  23.7 us (9%)
  local copies, waits for them, and re-layouts  17.5 us (6%)
  other arithmetic  16.1 us (6%)
  between operations  13.2 us (5%)
  loops' own time  5.53 us (2%)
    psum x1, waiting for transfers between devices, per_device(): raw_a, raw_b = lax.psum((part_a, part_b), 'ctx')  86.2 us
    reduce_scatter x1, waiting for transfers between devices, per_device(): lax.psum_scatter(make_term(lambda addend: addend, value_width), 'ctx', sc...  69.4 us
    all_gather x1, waiting for transfers between devices, per_device(): key_rows = lax.all_gather(keys, 'ctx', axis=0, tiled=True)  39.7 us
    dot_general x4, matrix products, compute(): jnp.einsum('kgtc,tkgd->ckd', weights, grad_heads, preferred_element_type=...  11.4 us
    dot_general x4, matrix products, head_scores(): jnp.einsum('tkgd,ckd->kgtc', query_heads, key_block, preferred_element_ty...  7.7 us
    dynamic_update_slice x8, local copies, waits for them, and re-layouts, make_term(): unused_final, pieces = lax.scan(piece_step, 0, piece_items)  5.61 us
  transfers between devices with their start and end apart: 3, of which 3 were waited for; matrix products, arithmetic and copies ran while one was open for 3% of the time, Pallas kernels for 0%

commit v1 on v0

v1 whole, which is shorter than its diff:
```python
import functools
import math

import jax
import jax.numpy as jnp
from jax import lax
from jax.experimental import pallas as pl
from jax.experimental.pallas import tpu as pltpu
from jax.sharding import PartitionSpec as P

HEAD = 128
KV = 4
GROUP = 4
RANK = 128
FEAT = 32
DOCS = 4
BLOCK = 64
ROWS = 128
WIDE = GROUP * ROWS
VROWS = RANK + 2 * FEAT
ACC = VROWS + 16
FAR = -1e30
EPS = 1e-06
GAIN = math.log2(math.e) / math.sqrt(HEAD)
F32 = jnp.float32
BF16 = jnp.bfloat16
NT = (((1,), (1,)), ((), ()))


def split2(x):
    hi = x.astype(BF16)
    return hi, (x - hi.astype(F32)).astype(BF16)


def dot(a, b):
    return jnp.dot(a, b, preferred_element_type=F32)


def dot3(a, b_hi, b_lo):
    hi, lo = split2(a)
    return dot(hi, b_hi) + dot(lo, b_hi) + dot(hi, b_lo)


def kernel(
    n_dev,
    x_hbm, q_hbm, k_hbm, g_hbm, ad_hbm, au_hbm, ds_hbm, us_hbm, order, lengths,
    out_ref,
    x_v, q_v, k_v, g_v, ad_v, au_v, ds_v, us_v,
    kbuf, vbuf, qs, w_hi, w_lo, m_ref, acc, lr_t, partial, rbuf, fin, doc_rows,
    in_sem, ring_send, ring_recv, sib_send, sib_recv, ar_send, ar_recv,
):
    n = n_dev // 2
    half = n // 2
    me = lax.axis_index("ctx")
    core = lax.rem(me, 2)
    chip = me // 2
    fold = lax.rem(chip, 2)
    spot = (chip // 2) * (1 - 2 * fold) + fold * (n - 1)

    def device_at(place, which):
        side = place // half
        return 2 * (2 * (place * (1 - 2 * side) + side * (n - 1)) + side) + which

    ahead = device_at(lax.rem(spot + 1, n), core)
    behind = device_at(lax.rem(spot + n - 1, n), core)
    sibling = 2 * chip + 1 - core

    loads = [
        pltpu.make_async_copy(src, dst, in_sem.at[i])
        for i, (src, dst) in enumerate(
            [(k_hbm, k_v), (x_hbm, x_v), (ad_hbm, ad_v), (ds_hbm, ds_v),
             (q_hbm, q_v), (g_hbm, g_v), (au_hbm, au_v), (us_hbm, us_v)]
        )
    ]
    for load in loads:
        load.start()

    def part(slot, which, m):
        if m < 2:
            return kbuf.at[slot, pl.ds(2 * m, 2), which]
        return vbuf.at[slot, pl.ds((VROWS // 2) * (m - 2), VROWS // 2), pl.ds(ROWS * which, ROWS)]

    def ring(way, step, m):
        src, dst = (step, step + 1) if way == 0 else ((n - step) % n, n - step - 1)
        return pltpu.make_async_remote_copy(
            src_ref=part(src, 0, m), dst_ref=part(dst, 0, m),
            send_sem=ring_send.at[way, step, m], recv_sem=ring_recv.at[dst, m],
            device_id={"ctx": ahead if way == 0 else behind},
            device_id_type=pl.DeviceIdType.MESH,
        )

    def across(slot, m):
        return pltpu.make_async_remote_copy(
            src_ref=part(slot, 0, m), dst_ref=part(slot, 1, m),
            send_sem=sib_send.at[slot, m], recv_sem=sib_recv.at[slot, m],
            device_id={"ctx": sibling}, device_id_type=pl.DeviceIdType.MESH,
        )

    sent = []

    def launch(copy):
        copy.start()
        sent.append(copy)

    barrier = pltpu.get_barrier_semaphore()
    for peer in (ahead, behind, sibling):
        pl.semaphore_signal(
            barrier, inc=1, device_id={"ctx": peer}, device_id_type=pl.DeviceIdType.MESH
        )
    loads[0].wait()
    for g in range(KV):
        kbuf[0, g, 0] = k_v[:, g * HEAD:(g + 1) * HEAD]
    pl.semaphore_wait(barrier, 3)
    for m in (0, 1):
        launch(ring(0, 0, m))
        launch(ring(1, 0, m))
        launch(across(0, m))

    for load in loads[1:4]:
        load.wait()
    low = dot(x_v[...], ad_v[...])
    signs_a = (2 * ds_v[...] - 1).astype(F32).astype(BF16)
    proj = dot(x_v[...], signs_a)
    lr_t[...] = low.T
    proj_hi, proj_lo = split2(proj.T)
    for k in range(4):
        vbuf[0, k * 32:(k + 1) * 32, 0:ROWS] = lr_t[pl.ds(k, 32, stride=4), :].astype(BF16)
    vbuf[0, RANK:RANK + FEAT, 0:ROWS] = proj_hi
    vbuf[0, RANK + FEAT:VROWS, 0:ROWS] = proj_lo
    for m in (2, 3):
        launch(ring(0, 0, m))
        launch(ring(1, 0, m))
        launch(across(0, m))

    tail_row = lax.broadcasted_iota(jnp.int32, (16, 2 * ROWS), 0)
    ones = jnp.where(tail_row == 0, 1.0, 0.0).astype(BF16)
    for s in range(n):
        vbuf[s, VROWS:ACC, :] = ones
    m_ref[...] = jnp.full(m_ref.shape, FAR, F32)
    acc[...] = jnp.zeros(acc.shape, F32)

    end0 = lengths[0]
    end1 = end0 + lengths[1]
    end2 = end1 + lengths[2]

    def positions(first, second, index):
        return jnp.where(index < BLOCK, first * BLOCK + index, second * BLOCK + index - BLOCK)

    def document(pos):
        return (
            (pos >= end0).astype(jnp.int32)
            + (pos >= end1).astype(jnp.int32)
            + (pos >= end2).astype(jnp.int32)
        )

    here0, here1 = order[2 * me], order[2 * me + 1]
    down = lax.broadcasted_iota(jnp.int32, (ROWS, ROWS), 0)
    along = lax.broadcasted_iota(jnp.int32, (ROWS, ROWS), 1)
    doc_down = document(positions(here0, here1, down))
    pos_along = positions(here0, here1, along)
    doc_along = document(pos_along)
    low_along = jnp.where(
        doc_along == 0, 0, jnp.where(doc_along == 1, end0, jnp.where(doc_along == 2, end1, end2))
    )
    member_b = jnp.where(doc_down == along // FEAT, 1.0, 0.0)
    member_a = jnp.where(doc_along == down // FEAT, 1.0, 0.0)
    doc_rows[...] = member_a

    for load in loads[4:]:
        load.wait()
    for g in range(KV):
        for h in range(GROUP):
            lane = (g * GROUP + h) * HEAD
            qs[g, h * ROWS:(h + 1) * ROWS, :] = q_v[:, lane:lane + HEAD]
    signs_b = (2 * us_v[...] - 1).astype(F32).astype(BF16)
    signs_b = jnp.concatenate([signs_b] * DOCS, axis=1)
    for g in range(KV):
        up_g = au_v[:, g * HEAD:(g + 1) * HEAD]
        sign_g = signs_b[g * HEAD:(g + 1) * HEAD, :]
        for h in range(GROUP):
            lane = (g * GROUP + h) * HEAD
            grad = g_v[:, lane:lane + HEAD]
            rows = slice(h * ROWS, (h + 1) * ROWS)
            a_hi, a_lo = split2(lax.dot_general(grad, up_g, NT, preferred_element_type=F32))
            b_hi, b_lo = split2(dot(grad, sign_g) * member_b)
            w_hi[g, rows, 0:RANK] = a_hi
            w_lo[g, rows, 0:RANK] = a_lo
            w_hi[g, rows, RANK:2 * RANK] = b_hi
            w_lo[g, rows, RANK:2 * RANK] = b_lo

    def chunk(slot):
        for m in range(4):
            across(slot, m).wait_recv()
        origin = device_at(lax.rem(spot + n - slot, n), 0)
        bias = []
        for which in (0, 1):
            source = origin + core * (1 - 2 * which) + which
            pos = positions(order[2 * source], order[2 * source + 1], down)
            allowed = (pos <= pos_along) & (pos >= low_along)
            bias.append(jnp.where(allowed, 0.0, FAR))
        bias = jnp.concatenate(bias, axis=0)
        bias = jnp.concatenate([bias] * GROUP, axis=1)

        def one(g, carry):
            keys = kbuf[slot, g].reshape(2 * ROWS, HEAD)
            scores = lax.dot_general(keys, qs[g], NT, preferred_element_type=F32) + bias
            before = m_ref[g]
            top = jnp.maximum(before, jnp.max(scores, axis=0, keepdims=True))
            weights = jnp.exp2((scores - top) * GAIN).astype(BF16)
            shrink = jnp.exp2((before - top) * GAIN)
            m_ref[g] = top
            acc[g] = acc[g] * shrink + dot(vbuf[slot], weights)
            return carry

        lax.fori_loop(0, KV, one, 0)

    pending = [0]
    for s in range(1, half):
        work = list(pending)
        for m in range(4):
            for way in (0, 1):
                slot = s if way == 0 else n - s
                ring(way, s - 1, m).wait_recv()
                if s < half - 1 or m % 2 == way:
                    launch(ring(way, s, m))
                launch(across(slot, m))
            if m % 2 == 1 and work:
                chunk(work.pop(0))
        for slot in work:
            chunk(slot)
        pending = [s, n - s]
    chunk(pending[0])
    for m in range(4):
        ring(m % 2, half - 1, m).wait_recv()
        launch(across(half, m))
    chunk(pending[1])
    chunk(half)

    raw_a = jnp.zeros((DOCS * FEAT, RANK), F32)
    raw_b = jnp.zeros((RANK, DOCS * FEAT), F32)
    for g in range(KV):
        scaled = acc[g, 0:VROWS, :] / acc[g, VROWS:VROWS + 1, :]
        left = scaled[RANK:RANK + FEAT] + scaled[RANK + FEAT:VROWS]
        left = jnp.concatenate([left] * DOCS, axis=0)
        left = left * jnp.concatenate([doc_rows[...]] * GROUP, axis=1)
        raw_a = raw_a + dot3(left, w_hi[g, :, 0:RANK], w_lo[g, :, 0:RANK])
        raw_b = raw_b + dot3(
            scaled[0:RANK], w_hi[g, :, RANK:2 * RANK], w_lo[g, :, RANK:2 * RANK]
        )
    partial[0:ROWS, :] = raw_a
    for d in range(DOCS):
        partial[ROWS + d * FEAT:ROWS + (d + 1) * FEAT, :] = jnp.concatenate(
            [raw_b[k * 32:(k + 1) * 32, d * FEAT:(d + 1) * FEAT] for k in range(4)], axis=1
        )

    piece = 2 * ROWS // n_dev

    def rows_of(device):
        return pl.ds(pl.multiple_of(device * piece, piece), piece)

    def scatter(k):
        peer = lax.rem(me + k, n_dev)
        return pltpu.make_async_remote_copy(
            src_ref=partial.at[rows_of(peer)], dst_ref=rbuf.at[k],
            send_sem=ar_send.at[0, k], recv_sem=ar_recv.at[0, k],
            device_id={"ctx": peer}, device_id_type=pl.DeviceIdType.MESH,
        )

    def spread(k):
        peer = lax.rem(me + k, n_dev)
        return pltpu.make_async_remote_copy(
            src_ref=fin.at[me], dst_ref=fin.at[me],
            send_sem=ar_send.at[1, k], recv_sem=ar_recv.at[1, k],
            device_id={"ctx": peer}, device_id_type=pl.DeviceIdType.MESH,
        )

    def arrival(k):
        source = lax.rem(me + n_dev - k, n_dev)
        return pltpu.make_async_remote_copy(
            src_ref=fin.at[source], dst_ref=fin.at[source],
            send_sem=ar_send.at[1, k], recv_sem=ar_recv.at[1, k],
            device_id={"ctx": lax.rem(me + k, n_dev)}, device_id_type=pl.DeviceIdType.MESH,
        )

    for k in range(1, n_dev):
        scatter(k).start()
    rbuf[0] = partial[rows_of(me), :]
    for k in range(1, n_dev):
        scatter(k).wait_recv()
    fin[me] = jnp.sum(rbuf[...], axis=0)
    for k in range(1, n_dev):
        spread(k).start()
    for k in range(1, n_dev):
        arrival(k).wait_recv()
    whole = fin[...].reshape(2 * DOCS, FEAT, RANK)
    mean = jnp.sum(
        jnp.sum(whole * whole, axis=1, keepdims=True), axis=2, keepdims=True
    ) * (1.0 / (FEAT * RANK))
    out_ref[...] = (whole * lax.rsqrt(mean + EPS)).reshape(2 * ROWS, RANK)
    for copy in sent:
        copy.wait_send()
    for k in range(1, n_dev):
        scatter(k).wait_send()
        spread(k).wait_send()


def per_device(n_dev, x, q, k, g, ad, au, ds, us, order, lengths):
    n = n_dev // 2
    anywhere = pl.BlockSpec(memory_space=pl.ANY)
    scalars = pl.BlockSpec(memory_space=pltpu.SMEM)
    dma = pltpu.SemaphoreType.DMA
    vmem = pltpu.VMEM
    out = pl.pallas_call(
        functools.partial(kernel, n_dev),
        out_shape=jax.ShapeDtypeStruct((2 * ROWS, RANK), F32),
        in_specs=[anywhere] * 8 + [scalars] * 2,
        out_specs=pl.BlockSpec(memory_space=pltpu.VMEM),
        scratch_shapes=[vmem(a.shape, a.dtype) for a in (x, q, k, g, ad, au, ds, us)]
        + [
            vmem((n, KV, 2, ROWS, HEAD), BF16),
            vmem((n, ACC, 2 * ROWS), BF16),
            vmem((KV, WIDE, HEAD), BF16),
            vmem((KV, WIDE, 2 * RANK), BF16),
            vmem((KV, WIDE, 2 * RANK), BF16),
            vmem((KV, 1, WIDE), F32),
            vmem((KV, ACC, WIDE), F32),
            vmem((RANK, ROWS), F32),
            vmem((2 * ROWS, RANK), F32),
            vmem((n_dev, 2 * ROWS // n_dev, RANK), F32),
            vmem((n_dev, 2 * ROWS // n_dev, RANK), F32),
            vmem((ROWS, ROWS), F32),
            dma((8,)),
            dma((2, n // 2, 4)),
            dma((n, 4)),
            dma((n, 4)),
            dma((n, 4)),
            dma((2, n_dev)),
            dma((2, n_dev)),
        ],
        compiler_params=pltpu.CompilerParams(
            collective_id=0, has_side_effects=True, vmem_limit_bytes=40 * 1024 * 1024
        ),
    )(x, q, k, g, ad, au, ds, us, order, lengths)
    out = out.reshape(2, DOCS, FEAT * RANK)
    return jnp.concatenate([out[0], out[1]], axis=1)


def solution(mesh):
    rows = P(("groups", "ctx"), None)
    placed = (rows, rows, rows, rows, P(), P(), P(), P(), P("groups"), P("groups"))
    return jax.shard_map(
        functools.partial(per_device, mesh.shape["ctx"]),
        mesh=mesh, in_specs=placed, out_specs=P("groups", None), check_vma=False,
    )
```

time: 274 us -> 50 us (0.18)
  waiting for transfers between devices: 196 us -> 0 us
  Pallas kernels: 0 us -> 42 us
  matrix products: 23.7 us -> 0 us
  other arithmetic: 16.1 us -> 0.69 us
  between operations: 13.2 us -> 0.09 us
  local copies, waits for them, and re-layouts: 17.5 us -> 6.99 us
  loops' own time: 5.53 us -> 0 us
    psum x1 -> x0, waiting for transfers between devices: 86.2 us -> none  [per_device(): raw_a, raw_b = lax.psum((part_a, part_b), 'ctx')]
    reduce_scatter x1 -> x0, waiting for transfers between devices: 69.4 us -> none  [per_device(): lax.psum_scatter(make_term(lambda addend: addend, value_width), 'ctx', sc...]
    pallas_call x0 -> x1, Pallas kernels: none -> 42 us  [per_device(): pl.pallas_call(functools.partial(kernel, n_dev), out_shape=jax.ShapeDtype...]
    all_gather x1 -> x0, waiting for transfers between devices: 39.7 us -> none  [per_device(): key_rows = lax.all_gather(keys, 'ctx', axis=0, tiled=True)]
    dot_general x14 -> x0, matrix products: 23.7 us -> none  [the longest x4 11.4 us: compute(): jnp.einsum('kgtc,tkgd->ckd', weights, grad_heads, preferred_element_type=...]
    reduce_or x8 -> x0, other arithmetic: 7.03 us -> none  [the longest x4 3.66 us: piece_step(): return (unused_carry, lax.cond(jnp.any(allowed), compute, empty, 0))]
    dynamic_update_slice x8 -> x0, local copies, waits for them, and re-layouts: 5.61 us -> none  [make_term(): unused_final, pieces = lax.scan(piece_step, 0, piece_items)]
    reduce_sum x8 -> x0, other arithmetic: 5.55 us -> none  [the longest x4 3.49 us: update(): jnp.sum(jnp.where(allowed, jnp.exp(score_block - new_top[..., None]), 0.0...]
  transfers between devices with their start and end apart: 3 -> 0, of which waited for: 3 -> 0; matrix products, arithmetic and copies ran while one was open for 3% -> 0% of each run, Pallas kernels for 0% -> 0%
where the time goes in v1:
time: 50 us; the launch traced here: 49.7 us
  Pallas kernels  42 us (84%)
  local copies, waits for them, and re-layouts  6.99 us (14%)
  other arithmetic  0.69 us (1%)
    pallas_call x1, Pallas kernels, per_device(): pl.pallas_call(functools.partial(kernel, n_dev), out_shape=jax.ShapeDtype...  42 us
    unnamed x18, local copies, waits for them, and re-layouts  6.92 us

profile of v1, /device:TPU:0, one launch (start us, length us, event | category | flops | bytes accessed | tf_op | source)
XLA Modules:
  0.0 49.7 jit_solution(9364110746890564014)
XLA Ops:
  0.0 0.0 copy-start.7
  0.0 0.0 copy-start.6
  0.0 0.0 copy-start.4
  0.0 0.0 copy-start
  0.0 1.1 %copy.12.us_hbm = s32[512,32]{1,0:T(8,128)S(1)} copy(s32[512,32]{0,1:T(8,128)} %param.17) | data formatting | bytes 131072 | tf_op args[7]
  1.1 1.6 %copy.11.ds_hbm = s32[4096,32]{1,0:T(8,128)S(1)} copy(s32[4096,32]{0,1:T(8,128)} %param.16) | data formatting | bytes 1048576 | tf_op args[6]
  2.7 0.0 copy-done.7
  2.7 0.0 copy-done.6
  2.7 0.0 copy-done.4
  2.8 0.0 copy-done
  2.8 0.0 copy-start.1
  2.8 1.2 %copy-done.1 = bf16[4096,128]{1,0:T(8,128)(2,1)S(1)} copy-done((bf16[4096,128]{1,0:T(8,128)(2,1)S(1)}, bf16[4096,128]{1,0:T(8,128)(2,1)}, u32[]{:S(2)}) %copy-start.1) | copy-done | bytes 1048600
  4.0 0.0 copy-start.2
  4.0 1.0 %copy-done.2 = bf16[128,2048]{1,0:T(8,128)(2,1)S(1)} copy-done((bf16[128,2048]{1,0:T(8,128)(2,1)S(1)}, bf16[128,2048]{1,0:T(8,128)(2,1)}, u32[]{:S(2)}) %copy-start.2) | copy-done | bytes 524312
  5.0 0.0 copy-start.3
  5.0 1.0 %copy-done.3 = bf16[128,2048]{1,0:T(8,128)(2,1)S(1)} copy-done((bf16[128,2048]{1,0:T(8,128)(2,1)S(1)}, bf16[128,2048]{1,0:T(8,128)(2,1)}, u32[]{:S(2)}) %copy-start.3) | copy-done | bytes 524312
  6.1 0.0 copy-start.5
  6.1 0.9 %copy-done.5 = bf16[128,512]{1,0:T(8,128)(2,1)S(1)} copy-done((bf16[128,512]{1,0:T(8,128)(2,1)S(1)}, bf16[128,512]{1,0:T(8,128)(2,1)}, u32[]{:S(2)}) %copy-start.5) | copy-done | bytes 131096
  7.0 42.0 %shard_map.100 = f32[256,128]{1,0:T(8,128)S(1)} custom-call(bf16[128,4096]{1,0:T(8,128)(2,1)S(1)} %copy-done, bf16[128,2048]{1,0:T(8,128)(2,1)S(1)} %copy-done.2, bf16[128,512]{1,0:T(8,128)(2,1)S(1)} %copy-done.4, bf16[128,2048]{1,0:T(8,128)(2,1)S(1)} %copy-done.3, bf16[4096,128]{1,0:T(8,128)(2,1)S(1)} %copy-done.1, bf16[128,512]{1,0:T(8,128)(2,1)S(1)} %copy-done.5, ...), custom_call_target="tpu_custom_call" | custom-call | tf_op jit(solution)/shard_map/pallas_call | solution.py:313
  49.1 0.7 %pad_maximum_fusion = f32[4,8192]{1,0:T(4,128)} fusion(f32[4,4096]{1,0:T(4,128)S(1)} %squeeze.7, f32[4,4096]{1,0:T(4,128)S(1)} %squeeze.6), kind=kLoop, calls=%fused_computation | loop fusion | flops 32768 | bytes 262144 | tf_op jit(solution)/shard_map/concatenate | solution.py:345
  (3 shorter events, 0.1 us)
Async XLA Ops:
  0.0 2.7 %copy-start.7 = (s32[4]{0:T(128)S(1)}, s32[4]{0:T(128)}, u32[]{:S(2)}) copy-start(s32[4]{0:T(128)} %lengths.1) | copy-start | bytes 52
  0.0 2.7 %copy-start.6 = (s32[32]{0:T(128)S(1)}, s32[32]{0:T(128)}, u32[]{:S(2)}) copy-start(s32[32]{0:T(128)} %order.1) | copy-start | bytes 388
  0.0 2.7 %copy-start.4 = (bf16[128,512]{1,0:T(8,128)(2,1)S(1)}, bf16[128,512]{1,0:T(8,128)(2,1)}, u32[]{:S(2)}) copy-start(bf16[128,512]{1,0:T(8,128)(2,1)} %k_hbm.1) | copy-start | bytes 393220
  0.0 2.8 %copy-start = (bf16[128,4096]{1,0:T(8,128)(2,1)S(1)}, bf16[128,4096]{1,0:T(8,128)(2,1)}, u32[]{:S(2)}) copy-start(bf16[128,4096]{1,0:T(8,128)(2,1)} %x_hbm.1) | copy-start | bytes 3145732
  2.8 1.2 %copy-start.1 = (bf16[4096,128]{1,0:T(8,128)(2,1)S(1)}, bf16[4096,128]{1,0:T(8,128)(2,1)}, u32[]{:S(2)}) copy-start(bf16[4096,128]{1,0:T(8,128)(2,1)} %ad_hbm.1) | copy-start | bytes 3145732
  4.0 1.0 %copy-start.2 = (bf16[128,2048]{1,0:T(8,128)(2,1)S(1)}, bf16[128,2048]{1,0:T(8,128)(2,1)}, u32[]{:S(2)}) copy-start(bf16[128,2048]{1,0:T(8,128)(2,1)} %q_hbm.1) | copy-start | bytes 1572868
  5.0 1.0 %copy-start.3 = (bf16[128,2048]{1,0:T(8,128)(2,1)S(1)}, bf16[128,2048]{1,0:T(8,128)(2,1)}, u32[]{:S(2)}) copy-start(bf16[128,2048]{1,0:T(8,128)(2,1)} %g_hbm.1) | copy-start | bytes 1572868
  6.1 0.9 %copy-start.5 = (bf16[128,512]{1,0:T(8,128)(2,1)S(1)}, bf16[128,512]{1,0:T(8,128)(2,1)}, u32[]{:S(2)}) copy-start(bf16[128,512]{1,0:T(8,128)(2,1)} %au_hbm.1) | copy-start | bytes 393220

commit v2 on v1

--- a/solution.py
+++ b/solution.py
@@ -120,9 +120,9 @@
         load.wait()
     low = dot(x_v[...], ad_v[...])
     signs_a = (2 * ds_v[...] - 1).astype(F32).astype(BF16)
-    proj = dot(x_v[...], signs_a)
+    proj = lax.dot_general(signs_a, x_v[...], NT, preferred_element_type=F32)
     lr_t[...] = low.T
-    proj_hi, proj_lo = split2(proj.T)
+    proj_hi, proj_lo = split2(proj)
     for k in range(4):
         vbuf[0, k * 32:(k + 1) * 32, 0:ROWS] = lr_t[pl.ds(k, 32, stride=4), :].astype(BF16)
     vbuf[0, RANK:RANK + FEAT, 0:ROWS] = proj_hi
@@ -172,68 +172,84 @@
         for h in range(GROUP):
             lane = (g * GROUP + h) * HEAD
             qs[g, h * ROWS:(h + 1) * ROWS, :] = q_v[:, lane:lane + HEAD]
-    signs_b = (2 * us_v[...] - 1).astype(F32).astype(BF16)
-    signs_b = jnp.concatenate([signs_b] * DOCS, axis=1)
-    for g in range(KV):
-        up_g = au_v[:, g * HEAD:(g + 1) * HEAD]
-        sign_g = signs_b[g * HEAD:(g + 1) * HEAD, :]
-        for h in range(GROUP):
-            lane = (g * GROUP + h) * HEAD
-            grad = g_v[:, lane:lane + HEAD]
-            rows = slice(h * ROWS, (h + 1) * ROWS)
-            a_hi, a_lo = split2(lax.dot_general(grad, up_g, NT, preferred_element_type=F32))
-            b_hi, b_lo = split2(dot(grad, sign_g) * member_b)
-            w_hi[g, rows, 0:RANK] = a_hi
-            w_lo[g, rows, 0:RANK] = a_lo
-            w_hi[g, rows, RANK:2 * RANK] = b_hi
-            w_lo[g, rows, RANK:2 * RANK] = b_lo
-
-    def chunk(slot):
-        for m in range(4):
-            across(slot, m).wait_recv()
-        origin = device_at(lax.rem(spot + n - slot, n), 0)
-        bias = []
-        for which in (0, 1):
-            source = origin + core * (1 - 2 * which) + which
-            pos = positions(order[2 * source], order[2 * source + 1], down)
-            allowed = (pos <= pos_along) & (pos >= low_along)
-            bias.append(jnp.where(allowed, 0.0, FAR))
-        bias = jnp.concatenate(bias, axis=0)
-        bias = jnp.concatenate([bias] * GROUP, axis=1)
+    def weigh():
+        signs_b = (2 * us_v[...] - 1).astype(F32).astype(BF16)
+        signs_b = jnp.concatenate([signs_b] * DOCS, axis=0)
+        for g in range(KV):
+            up_g = au_v[:, g * HEAD:(g + 1) * HEAD]
+            sign_g = signs_b[:, g * HEAD:(g + 1) * HEAD]
+            for h in range(GROUP):
+                lane = (g * GROUP + h) * HEAD
+                grad = g_v[:, lane:lane + HEAD]
+                rows = slice(h * ROWS, (h + 1) * ROWS)
+                a_hi, a_lo = split2(lax.dot_general(grad, up_g, NT, preferred_element_type=F32))
+                b_hi, b_lo = split2(
+                    lax.dot_general(grad, sign_g, NT, preferred_element_type=F32) * member_b
+                )
+                w_hi[g, rows, 0:RANK] = a_hi
+                w_lo[g, rows, 0:RANK] = a_lo
+                w_hi[g, rows, RANK:2 * RANK] = b_hi
+                w_lo[g, rows, RANK:2 * RANK] = b_lo
+
+    def chunk(*slots):
+        biases = []
+        for slot in slots:
+            for m in range(4):
+                across(slot, m).wait_recv()
+            origin = device_at(lax.rem(spot + n - slot, n), 0)
+            bias = []
+            for which in (0, 1):
+                source = origin + core * (1 - 2 * which) + which
+                pos = positions(order[2 * source], order[2 * source + 1], down)
+                allowed = (pos <= pos_along) & (pos >= low_along)
+                bias.append(jnp.where(allowed, 0.0, FAR))
+            bias = jnp.concatenate(bias, axis=0)
+            biases.append(jnp.concatenate([bias] * GROUP, axis=1))
 
         def one(g, carry):
-            keys = kbuf[slot, g].reshape(2 * ROWS, HEAD)
-            scores = lax.dot_general(keys, qs[g], NT, preferred_element_type=F32) + bias
             before = m_ref[g]
-            top = jnp.maximum(before, jnp.max(scores, axis=0, keepdims=True))
-            weights = jnp.exp2((scores - top) * GAIN).astype(BF16)
+            top = before
+            scores = []
+            for slot, bias in zip(slots, biases):
+                keys = kbuf[slot, g].reshape(2 * ROWS, HEAD)
+                part_scores = lax.dot_general(keys, qs[g], NT, preferred_element_type=F32) + bias
+                scores.append(part_scores)
+                top = jnp.maximum(top, jnp.max(part_scores, axis=0, keepdims=True))
             shrink = jnp.exp2((before - top) * GAIN)
             m_ref[g] = top
-            acc[g] = acc[g] * shrink + dot(vbuf[slot], weights)
+            total = acc[g] * shrink
+            for slot, part_scores in zip(slots, scores):
+                weights = jnp.exp2((part_scores - top) * GAIN).astype(BF16)
+                total = total + dot(vbuf[slot], weights)
+            acc[g] = total
             return carry
 
-        lax.fori_loop(0, KV, one, 0)
+        lax.fori_loop(0, KV, one, 0, unroll=True)
+
+    def pass_on(s, m):
+        for way in (0, 1):
+            ring(way, s - 1, m).wait_recv()
+            if s < half - 1 or m % 2 == way:
+                launch(ring(way, s, m))
+        for slot in (s, n - s):
+            launch(across(slot, m))
 
     pending = [0]
     for s in range(1, half):
-        work = list(pending)
-        for m in range(4):
-            for way in (0, 1):
-                slot = s if way == 0 else n - s
-                ring(way, s - 1, m).wait_recv()
-                if s < half - 1 or m % 2 == way:
-                    launch(ring(way, s, m))
-                launch(across(slot, m))
-            if m % 2 == 1 and work:
-                chunk(work.pop(0))
-        for slot in work:
-            chunk(slot)
+        for m in (0, 1):
+            pass_on(s, m)
+        chunk(*pending[:1])
+        for m in (2, 3):
+            pass_on(s, m)
+        if s == 1:
+            weigh()
+        else:
+            chunk(*pending[1:])
         pending = [s, n - s]
-    chunk(pending[0])
     for m in range(4):
         ring(m % 2, half - 1, m).wait_recv()
         launch(across(half, m))
-    chunk(pending[1])
+    chunk(*pending)
     chunk(half)
 
     raw_a = jnp.zeros((DOCS * FEAT, RANK), F32)
@@ -306,6 +322,7 @@
 
 def per_device(n_dev, x, q, k, g, ad, au, ds, us, order, lengths):
     n = n_dev // 2
+    ds, us = ds.T, us.T
     anywhere = pl.BlockSpec(memory_space=pl.ANY)
     scalars = pl.BlockSpec(memory_space=pltpu.SMEM)
     dma = pltpu.SemaphoreType.DMA
@@ -338,7 +355,7 @@
             dma((2, n_dev)),
         ],
         compiler_params=pltpu.CompilerParams(
-            collective_id=0, has_side_effects=True, vmem_limit_bytes=40 * 1024 * 1024
+            collective_id=0, has_side_effects=True, vmem_limit_bytes=60 * 1024 * 1024
         ),
     )(x, q, k, g, ad, au, ds, us, order, lengths)
     out = out.reshape(2, DOCS, FEAT * RANK)

time: 50 us -> 41 us (0.82)
  local copies, waits for them, and re-layouts: 6.99 us -> 0.94 us
  Pallas kernels: 42 us -> 39.2 us
    unnamed x18 -> x0, local copies, waits for them, and re-layouts: 6.92 us -> none
    pallas_call x1, Pallas kernels: 42 us -> 39.2 us  [per_device(): pl.pallas_call(functools.partial(kernel, n_dev), out_shape=jax.ShapeDtype...]
    slice x1, local copies, waits for them, and re-layouts: 0.01 us -> 0.88 us  [per_device(): return jnp.concatenate([out[0], out[1]], axis=1)]
where the time goes in v2:
time: 41 us; the launch traced here: 40.8 us
  Pallas kernels  39.2 us (96%)
  local copies, waits for them, and re-layouts  0.94 us (2%)
  other arithmetic  0.69 us (2%)
    pallas_call x1, Pallas kernels, per_device(): pl.pallas_call(functools.partial(kernel, n_dev), out_shape=jax.ShapeDtype...  39.2 us
    slice x1, local copies, waits for them, and re-layouts, per_device(): return jnp.concatenate([out[0], out[1]], axis=1)  0.88 us

profile of v2, /device:TPU:0, one launch (start us, length us, event | category | flops | bytes accessed | tf_op | source)
XLA Modules:
  0.0 40.8 jit_solution(14629842760402934124)
XLA Ops:
  0.0 39.2 %shard_map.100 = f32[256,128]{1,0:T(8,128)} custom-call(bf16[128,4096]{1,0:T(8,128)(2,1)} %x_hbm.1, bf16[128,2048]{1,0:T(8,128)(2,1)} %q_hbm.1, bf16[128,512]{1,0:T(8,128)(2,1)} %k_hbm.1, bf16[128,2048]{1,0:T(8,128)(2,1)} %g_hbm.1, bf16[4096,128]{1,0:T(8,128)(2,1)} %ad_hbm.1, bf16[128,512]{1,0:T(8,128)(2,1)} %au_hbm.1, s32[32,4096]{1,0:T(8,128)} %bitcast.2, ...), custom_call_target="tpu_custom_call" | custom-call | tf_op jit(solution)/shard_map/pallas_call | solution.py:330
  39.2 0.9 %fusion = (f32[128,128]{1,0:T(8,128)S(1)}, f32[128,128]{1,0:T(8,128)S(1)}) fusion(f32[256,128]{1,0:T(8,128)} %shard_map.100), kind=kLoop, calls=%fused_computation.1 | loop fusion | bytes 262144 | tf_op jit(solution)/shard_map/slice | solution.py:362
  40.1 0.7 %pad_maximum_fusion = f32[4,8192]{1,0:T(4,128)} fusion(f32[4,4096]{1,0:T(4,128)S(1)} %squeeze.7, f32[4,4096]{1,0:T(4,128)S(1)} %squeeze.6), kind=kLoop, calls=%fused_computation | loop fusion | flops 32768 | bytes 262144 | tf_op jit(solution)/shard_map/concatenate | solution.py:362
  (2 shorter events, 0.1 us)

commit v3 on v2

--- a/solution.py
+++ b/solution.py
@@ -238,13 +238,11 @@
     for s in range(1, half):
         for m in (0, 1):
             pass_on(s, m)
-        chunk(*pending[:1])
         for m in (2, 3):
             pass_on(s, m)
+        chunk(*pending)
         if s == 1:
             weigh()
-        else:
-            chunk(*pending[1:])
         pending = [s, n - s]
     for m in range(4):
         ring(m % 2, half - 1, m).wait_recv()
@@ -301,22 +299,27 @@
     for k in range(1, n_dev):
         scatter(k).start()
     rbuf[0] = partial[rows_of(me), :]
+    for copy in sent:
+        copy.wait_send()
     for k in range(1, n_dev):
         scatter(k).wait_recv()
     fin[me] = jnp.sum(rbuf[...], axis=0)
     for k in range(1, n_dev):
         spread(k).start()
+    for k in range(1, n_dev):
+        scatter(k).wait_send()
     for k in range(1, n_dev):
         arrival(k).wait_recv()
     whole = fin[...].reshape(2 * DOCS, FEAT, RANK)
     mean = jnp.sum(
         jnp.sum(whole * whole, axis=1, keepdims=True), axis=2, keepdims=True
     ) * (1.0 / (FEAT * RANK))
-    out_ref[...] = (whole * lax.rsqrt(mean + EPS)).reshape(2 * ROWS, RANK)
-    for copy in sent:
-        copy.wait_send()
-    for k in range(1, n_dev):
-        scatter(k).wait_send()
+    partial[...] = (whole * lax.rsqrt(mean + EPS)).reshape(2 * ROWS, RANK)
+    for k in range(2):
+        for f in range(FEAT):
+            lane = (k * FEAT + f) * RANK
+            out_ref[:, lane:lane + RANK] = partial[pl.ds(k * ROWS + f, DOCS, stride=FEAT), :]
+    for k in range(1, n_dev):
         spread(k).wait_send()
 
 
@@ -327,9 +330,9 @@
     scalars = pl.BlockSpec(memory_space=pltpu.SMEM)
     dma = pltpu.SemaphoreType.DMA
     vmem = pltpu.VMEM
-    out = pl.pallas_call(
+    return pl.pallas_call(
         functools.partial(kernel, n_dev),
-        out_shape=jax.ShapeDtypeStruct((2 * ROWS, RANK), F32),
+        out_shape=jax.ShapeDtypeStruct((DOCS, 2 * FEAT * RANK), F32),
         in_specs=[anywhere] * 8 + [scalars] * 2,
         out_specs=pl.BlockSpec(memory_space=pltpu.VMEM),
         scratch_shapes=[vmem(a.shape, a.dtype) for a in (x, q, k, g, ad, au, ds, us)]
@@ -358,8 +361,6 @@
             collective_id=0, has_side_effects=True, vmem_limit_bytes=60 * 1024 * 1024
         ),
     )(x, q, k, g, ad, au, ds, us, order, lengths)
-    out = out.reshape(2, DOCS, FEAT * RANK)
-    return jnp.concatenate([out[0], out[1]], axis=1)
 
 
 def solution(mesh):

time: 41 us -> 40.3 us (0.983)
  Pallas kernels: 39.2 us -> 38.5 us
  other arithmetic: 0.69 us -> 0 us
  local copies, waits for them, and re-layouts: 0.94 us -> 1.57 us
    unnamed x0 -> x1, local copies, waits for them, and re-layouts: none -> 1.57 us
    slice x1 -> x0, local copies, waits for them, and re-layouts: 0.88 us -> none  [per_device(): return jnp.concatenate([out[0], out[1]], axis=1)]
    concatenate x1 -> x0, other arithmetic: 0.69 us -> none  [per_device(): return jnp.concatenate([out[0], out[1]], axis=1)]
    pallas_call x1, Pallas kernels: 39.2 us -> 38.5 us  [per_device(): pl.pallas_call(functools.partial(kernel, n_dev), out_shape=jax.ShapeDtype...]
where the time goes in v3:
time: 40.3 us; the launch traced here: 40.1 us
  Pallas kernels  38.5 us (96%)
  local copies, waits for them, and re-layouts  1.57 us (4%)
    pallas_call x1, Pallas kernels, per_device(): pl.pallas_call(functools.partial(kernel, n_dev), out_shape=jax.ShapeDtype...  38.5 us
    unnamed x1, local copies, waits for them, and re-layouts  1.57 us

profile of v3, /device:TPU:0, one launch (start us, length us, event | category | flops | bytes accessed | tf_op | source)
XLA Modules:
  0.0 40.1 jit_solution(6615149845032950549)
XLA Ops:
  0.0 38.5 %shard_map.100 = f32[4,8192]{1,0:T(4,128)} custom-call(bf16[128,4096]{1,0:T(8,128)(2,1)} %x_hbm.1, bf16[128,2048]{1,0:T(8,128)(2,1)} %q_hbm.1, bf16[128,512]{1,0:T(8,128)(2,1)} %k_hbm.1, bf16[128,2048]{1,0:T(8,128)(2,1)} %g_hbm.1, bf16[4096,128]{1,0:T(8,128)(2,1)} %ad_hbm.1, bf16[128,512]{1,0:T(8,128)(2,1)} %au_hbm.1, s32[32,4096]{1,0:T(8,128)} %bitcast.2, ...), custom_call_target="tpu_custom_call" | custom-call | tf_op jit(solution)/shard_map/pallas_call | solution.py:333
  38.5 1.6 %copy.12 = f32[4,8192]{1,0:T(4,128)} copy(f32[4,8192]{1,0:T(4,128)} %shard_map.100) | data formatting | bytes 262144

commit v4 on v3

--- a/solution.py
+++ b/solution.py
@@ -38,7 +38,8 @@
 
 def dot3(a, b_hi, b_lo):
     hi, lo = split2(a)
-    return dot(hi, b_hi) + dot(lo, b_hi) + dot(hi, b_lo)
+    both = dot(jnp.concatenate([hi, lo], axis=0), b_hi)
+    return both[:a.shape[0]] + both[a.shape[0]:] + dot(hi, b_lo)
 
 
 def kernel(

time: 40.3 us -> 40.2 us (level)
  no operation moved by 1% of the time
where the time goes in v4:
time: 40.2 us; the launch traced here: 40.1 us
  Pallas kernels  38.5 us (96%)
  local copies, waits for them, and re-layouts  1.57 us (4%)
    pallas_call x1, Pallas kernels, per_device(): pl.pallas_call(functools.partial(kernel, n_dev), out_shape=jax.ShapeDtype...  38.5 us
    unnamed x1, local copies, waits for them, and re-layouts  1.57 us

profile of v4, /device:TPU:0, one launch (start us, length us, event | category | flops | bytes accessed | tf_op | source)
XLA Modules:
  0.0 40.1 jit_solution(18384336639204922994)
XLA Ops:
  0.0 38.5 %shard_map.100 = f32[4,8192]{1,0:T(4,128)} custom-call(bf16[128,4096]{1,0:T(8,128)(2,1)} %x_hbm.1, bf16[128,2048]{1,0:T(8,128)(2,1)} %q_hbm.1, bf16[128,512]{1,0:T(8,128)(2,1)} %k_hbm.1, bf16[128,2048]{1,0:T(8,128)(2,1)} %g_hbm.1, bf16[4096,128]{1,0:T(8,128)(2,1)} %ad_hbm.1, bf16[128,512]{1,0:T(8,128)(2,1)} %au_hbm.1, s32[32,4096]{1,0:T(8,128)} %bitcast.2, ...), custom_call_target="tpu_custom_call" | custom-call | tf_op jit(solution)/shard_map/pallas_call | solution.py:334
  38.5 1.6 %copy.12 = f32[4,8192]{1,0:T(4,128)} copy(f32[4,8192]{1,0:T(4,128)} %shard_map.100) | data formatting | bytes 262144
